TPU v7x, 256 devices: a whole 4x4x8 slice. The times are simulated.
256 devices in a mesh: pool: 2 (over core), grp: 8 (over x_hi, y), tp: 16 (over x_lo, z).
Axes of the slice: x: 4 (x_hi: 2, x_lo: 2; x = x_hi * 2 + x_lo), y: 4, z: 8, core: 2. Of those that a mesh axis runs over, the one named last changes fastest.
Arguments:
- hidden_rows: bfloat16 [2, 8192, 8192], P('pool', ('grp', 'tp')), may hold values from -17 to 17
- w_query: bfloat16 [8192, 8192], P(None, 'tp'), may hold values from -0.0625 to 0.0625
- key_matrix: bfloat16 [8192, 1024], P(None, 'tp'), may hold values from -0.0625 to 0.0625
- value_matrix: bfloat16 [8192, 1024], P(None, 'tp'), may hold values from -0.0625 to 0.0625
- resident_cache: bfloat16 [4096, 16, 4096], P('grp', None, 'tp'), may hold values from -6 to 6
- page_req: int32 [512], P('grp'), may hold values from 0 to 64, as said below
- req_len: int32 [64], replicated, may hold values from 1 to 128, as said below
- assign: int32 [64], replicated, may hold values from 0 to 7, as said below
- row_src: int32 [2048], P('grp'), may hold values from 0 to 7
- resident_length: int32 [2048], P('grp'), may hold values from 1 to 32
- page_lookup: int32 [2048, 2], P('grp'), may hold values from 0 to 511, as said below
Outputs:
- attended: bfloat16 [2, 8192, 8192], P('pool', 'grp', 'tp')
Inputs may be any that keep to these rules, and one draw needn't show every extreme that they name: `page_req`: requests g * 8 to g * 8 + 7 belong to prefill group g and take its pages in that order from its first page, each 1 to 8 consecutive pages; the pages after them carry 64. `req_len`: A request of c pages has between (c - 1) * 16 + 1 and c * 16 tokens. `assign`: the 8 requests of one prefill group go to 8 different decode groups. `page_lookup`: the entries of all rows of one decode group are distinct.
All inputs are finite; a program needn't handle non-finite values.
Results may differ from a plain program's by a relative error of at most 0.012.
Values may be sent and summed in bfloat16 or wider, within the bound.
No kernel may reach another device: no remote copies, remote signals or barrier semaphores. Data moves between devices by JAX's collectives and lax.ppermute only.
A program may use at most 128 MiB of HBM per device.

v0:
```python
import functools
import math

import jax
import jax.numpy as jnp
from jax import lax
from jax.experimental import pallas as pl
from jax.experimental.pallas import tpu as pltpu
from jax.sharding import PartitionSpec as P

HEAD = 128
PAGE = 16
STEPS = 4
THETA = 500000.0
MASKED = -1e30
SCALE = HEAD**-0.5
RATE = SCALE / math.log(2.0)
KPART = 8
MODEL = 8192
KW = MODEL // KPART
RING = 8
SHARD = 64
QCOLS = 512
PIECE = KW + 256
GROUPS = 8
ROWS = 1024
DROWS = 256
HALF = 512
BIG = 63 << 20
BF = jnp.bfloat16
F32 = jnp.float32


def ring_y(step):
    return [(x * 4 + y, x * 4 + (y + step) % 4) for x in range(2) for y in range(4)]


def flip(mask):
    return [(t, t ^ mask) for t in range(16)]


def far_x():
    pairs = []
    for pool in range(2):
        for g in range(GROUPS):
            for t in range(16):
                x_hi, y = divmod(g, 4)
                x_lo, z = divmod(t, RING)
                x = x_hi * 2 + x_lo
                to = (x + 1) % 4 if x % 2 else (x - 1) % 4
                pairs.append(
                    (
                        (pool * GROUPS + g) * 16 + t,
                        (pool * GROUPS + (to // 2) * 4 + y) * 16 + (to % 2) * RING + z,
                    )
                )
    return pairs


def cut_kernel(offsets, query, key, value, *refs):
    first, second, sems = refs[-3:]
    copies = []
    for s, out in enumerate((first, second)):
        start = pl.multiple_of(offsets[s] * KW, KW)
        copies.append(
            pltpu.make_async_copy(query.at[pl.ds(start, KW), :], out.at[pl.ds(0, KW), :], sems.at[s, 0])
        )
        copies += tall_copies(key, value, start, out, sems.at[s])
    for copy in copies:
        copy.start()
    for copy in copies:
        copy.wait()


def tall_copies(key, value, start, out, sems):
    copies = []
    for run in range(2):
        for i, source in enumerate((key, value)):
            copies.append(
                pltpu.make_async_copy(
                    source.at[:, pl.ds(pl.multiple_of(start + run * QCOLS, QCOLS), QCOLS)],
                    out.at[pl.ds(KW + run * HEAD + i * SHARD, SHARD), :],
                    sems.at[1 + run * 2 + i],
                )
            )
    return copies


def cut(offsets, query, key, value, extra):
    anywhere = pl.BlockSpec(memory_space=pl.ANY)
    return pl.pallas_call(
        cut_kernel,
        out_shape=[jax.ShapeDtypeStruct((PIECE, QCOLS), BF)] * 2,
        in_specs=[pl.BlockSpec(memory_space=pltpu.SMEM)] + [anywhere] * (3 + len(extra)),
        out_specs=[pl.BlockSpec(memory_space=pltpu.VMEM)] * 2,
        scratch_shapes=[pltpu.SemaphoreType.DMA((2, 5))],
        compiler_params=pltpu.CompilerParams(vmem_limit_bytes=BIG),
        cost_estimate=pl.CostEstimate(flops=0, bytes_accessed=4 * PIECE * QCOLS * 2, transcendentals=0),
        name="cut",
    )(offsets, query, key, value, *extra)


def row_copies(order, rows, scratch, sems):
    return [
        pltpu.make_async_copy(
            rows.at[:, pl.ds(pl.multiple_of(order[k] * KW, KW), KW)], scratch.at[k], sems.at[k]
        )
        for k in range(KPART)
    ]


def tall_kernel(order, rows, key, value, *refs):
    pieces = refs[:KPART]
    own_out, side_out, xs, own_w, side_w, xsem, osem, ssem = refs[KPART:]
    x_copies = row_copies(order, rows, xs, xsem)
    copies = []
    for k in range(KPART):
        start = pl.multiple_of(order[k] * KW, KW)
        copies.append(
            [x_copies[k], pltpu.make_async_copy(pieces[k].at[pl.ds(KW, 2 * HEAD), :], side_w.at[k], ssem.at[k])]
            + [
                pltpu.make_async_copy(
                    source.at[:, pl.ds(start, KW)], own_w.at[k, pl.ds(i * SHARD, SHARD), :], osem.at[k, i]
                )
                for i, source in enumerate((key, value))
            ]
        )
        for copy in copies[k]:
            copy.start()
    dims = (((1,), (1,)), ((), ()))
    tall = None
    for k in range(KPART):
        for copy in copies[k]:
            copy.wait()
        weight = jnp.concatenate([side_w[k, :HEAD, :], side_w[k, HEAD:, :]], axis=1)
        both = lax.dot_general(
            xs[k], jnp.concatenate([own_w[k], weight], axis=0), dims, preferred_element_type=F32
        )
        tall = both if k == 0 else tall + both
    own_out[...] = tall[:, :HEAD].astype(BF)
    side_out[...] = tall[:, HEAD:].astype(BF)


def project_tall(order, rows, key, value, pieces):
    anywhere = pl.BlockSpec(memory_space=pl.ANY)
    return pl.pallas_call(
        tall_kernel,
        out_shape=[jax.ShapeDtypeStruct((HALF, HEAD), BF)] * 2,
        in_specs=[pl.BlockSpec(memory_space=pltpu.SMEM)] + [anywhere] * (3 + len(pieces)),
        out_specs=[pl.BlockSpec(memory_space=pltpu.VMEM)] * 2,
        scratch_shapes=[
            pltpu.VMEM((KPART, HALF, KW), BF),
            pltpu.VMEM((KPART, HEAD, KW), BF),
            pltpu.VMEM((KPART, 2 * HEAD, QCOLS), BF),
            pltpu.SemaphoreType.DMA((KPART,)),
            pltpu.SemaphoreType.DMA((KPART, 2)),
            pltpu.SemaphoreType.DMA((KPART,)),
        ],
        compiler_params=pltpu.CompilerParams(vmem_limit_bytes=BIG),
        cost_estimate=pl.CostEstimate(
            flops=4 * HALF * MODEL * HEAD, bytes_accessed=12 << 20, transcendentals=0
        ),
        name="project_tall",
    )(order, rows, key, value, *pieces)


def query_kernel(order, rows, *refs):
    weights = refs[:-5]
    out, xs, ws, xsem, wsem = refs[-5:]
    x_copies = row_copies(order, rows, xs, xsem)
    w_copies = []
    for k in range(KPART):
        w_copies.append(pltpu.make_async_copy(weights[k].at[pl.ds(0, KW), :], ws.at[k], wsem.at[k]))
        x_copies[k].start()
        w_copies[k].start()
    total = None
    for k in range(KPART):
        x_copies[k].wait()
        w_copies[k].wait()
        part = jnp.dot(xs[k], ws[k], preferred_element_type=F32)
        total = part if k == 0 else total + part
    out[...] = total.astype(BF)


def project_query(order, rows, weights):
    anywhere = pl.BlockSpec(memory_space=pl.ANY)
    return pl.pallas_call(
        query_kernel,
        out_shape=jax.ShapeDtypeStruct((HALF, QCOLS), BF),
        in_specs=[pl.BlockSpec(memory_space=pltpu.SMEM)] + [anywhere] * (1 + len(weights)),
        out_specs=pl.BlockSpec(memory_space=pltpu.VMEM),
        scratch_shapes=[
            pltpu.VMEM((KPART, HALF, KW), BF),
            pltpu.VMEM((KPART, KW, QCOLS), BF),
            pltpu.SemaphoreType.DMA((KPART,)),
            pltpu.SemaphoreType.DMA((KPART,)),
        ],
        compiler_params=pltpu.CompilerParams(vmem_limit_bytes=BIG),
        cost_estimate=pl.CostEstimate(
            flops=2 * HALF * MODEL * QCOLS, bytes_accessed=16 << 20, transcendentals=0
        ),
        name="project_query",
    )(order, rows, *weights)


def bring(sources, targets, sems):
    copies = [pltpu.make_async_copy(s, t, sems.at[i]) for i, (s, t) in enumerate(zip(sources, targets))]
    for copy in copies:
        copy.start()
    for copy in copies:
        copy.wait()


def swap_halves(value):
    return pltpu.roll(value, HEAD // 2, 1)


def keys_kernel(place, *refs):
    sources, (_, keys, values, bins), held, (halves, joined, sems) = refs[:6], refs[6:10], refs[10:16], refs[16:]
    own, pair, side, diag, cosine, sine = held
    bring(sources, held, sems)
    z, x_lo = place[0], place[1]
    odd = lax.rem(z, 2)
    for slot, mine, theirs in ((odd, own, side), (1 - odd, pair, diag)):
        halves[slot, pl.ds(pl.multiple_of(x_lo * HALF, HALF), HALF), :] = mine[...].astype(F32)
        halves[slot, pl.ds(pl.multiple_of((1 - x_lo) * HALF, HALF), HALF), :] = theirs[:, theirs.shape[1] - HEAD :].astype(F32)
    lower = lax.broadcasted_iota(jnp.int32, (ROWS, HEAD), 1) < HEAD // 2
    low, high = halves[0], halves[1]
    key = jnp.where(lower, low, swap_halves(high))
    value = jnp.where(lower, swap_halves(low), high).astype(BF)
    key = (key * cosine[...] + swap_halves(key) * sine[...]).astype(BF)
    keys[...] = key
    values[...] = value
    joined[pl.ds(0, ROWS), pl.ds(0, HEAD)] = key
    joined[pl.ds(0, ROWS), pl.ds(HEAD, HEAD)] = value
    joined[pl.ds(ROWS, HEAD), :] = jnp.zeros((HEAD, 2 * HEAD), BF)
    for c in range(GROUPS):
        start = pl.multiple_of(place[2 + c] * PAGE, PAGE)
        bins[c] = jnp.zeros((HEAD, 2 * HEAD), BF)
        bins[GROUPS + c] = joined[pl.ds(start, HEAD), :]


def make_keys(place, after, *arrays):
    outs = [
        jax.ShapeDtypeStruct((ROWS, HEAD), BF),
        jax.ShapeDtypeStruct((ROWS, HEAD), BF),
        jax.ShapeDtypeStruct((2 * GROUPS, HEAD, 2 * HEAD), BF),
    ]
    vm, anywhere = pl.BlockSpec(memory_space=pltpu.VMEM), pl.BlockSpec(memory_space=pl.ANY)
    return pl.pallas_call(
        keys_kernel,
        out_shape=outs,
        in_specs=[pl.BlockSpec(memory_space=pltpu.SMEM)] + [anywhere] * (len(arrays) + 1),
        out_specs=[vm] * 3,
        scratch_shapes=[
            *[pltpu.VMEM(x.shape, x.dtype) for x in arrays],
            pltpu.VMEM((2, ROWS, HEAD), F32),
            pltpu.VMEM((ROWS + HEAD, 2 * HEAD), BF),
            pltpu.SemaphoreType.DMA((len(arrays),)),
        ],
        compiler_params=pltpu.CompilerParams(vmem_limit_bytes=BIG),
        cost_estimate=pl.CostEstimate(flops=1 << 33, bytes_accessed=4 << 20, transcendentals=0),
        name="keys",
    )(place, *arrays, after)


def attend_kernel(place, lookup, order, rows, weights, *refs):
    sources, (out, acc_out, level), held, rest = refs[:9], refs[9:12], refs[12:21], refs[21:]
    xs, ws, queries, acc, fresh_k, fresh_v, xsem, wsem, sems = rest
    side, cosine, sine, keys, values, stored_bias, seen, usable, cache = held
    z, x_lo, pool = place[0], place[1], place[10]
    x_copies = row_copies(order, rows, xs, xsem)
    w_copies = [
        pltpu.make_async_copy(
            weights.at[pl.ds(pl.multiple_of(order[k] * KW, KW), KW), :], ws.at[k], wsem.at[k]
        )
        for k in range(KPART)
    ]
    copies = [pltpu.make_async_copy(sources[i], held[i], sems.at[i]) for i in range(9)]
    for k in range(KPART):
        x_copies[k].start()
        w_copies[k].start()
    for copy in copies:
        copy.start()
    own = None
    for k in range(KPART):
        x_copies[k].wait()
        w_copies[k].wait()
        part = jnp.dot(xs[k], ws[k], preferred_element_type=F32)
        own = part if k == 0 else own + part
    for copy in copies:
        copy.wait()
    for array, lo in ((own, x_lo), (side, 1 - x_lo)):
        here = pl.ds(pl.multiple_of(lo * HALF, HALF), HALF)
        c, s = cosine[here, :], sine[here, :]
        for h in range(4):
            lanes = slice(h * HEAD, (h + 1) * HEAD)
            q = array[:, lanes].astype(F32)
            q = q * c + swap_halves(q) * s
            queries[here, lanes] = q.astype(BF).astype(F32)
    dims = (((1,), (1,)), ((), ()))

    @pl.when(pool == 0)
    def _():
        fresh_k[pl.ds(0, HEAD), :] = jnp.zeros((HEAD, HEAD), F32)
        fresh_v[pl.ds(0, HEAD), :] = jnp.zeros((HEAD, HEAD), F32)
        fresh_k[pl.ds(HEAD, ROWS), :] = keys[...].astype(F32)
        fresh_v[pl.ds(HEAD, ROWS), :] = values[...].astype(F32)

        def block(b, carry):
            start = pl.multiple_of(b * HEAD, HEAD)
            k = fresh_k[pl.ds(start, 2 * HEAD), :].astype(BF)
            v = fresh_v[pl.ds(start, 2 * HEAD), :].astype(BF)
            bias = seen[b]
            keep = usable[pl.ds(start, HEAD), :]
            for h in range(4):
                q = queries[pl.ds(start, HEAD), h * HEAD : (h + 1) * HEAD].astype(BF)
                score = lax.dot_general(q, k, dims, preferred_element_type=F32) + bias
                peak = jnp.max(score, axis=1, keepdims=True)
                p = jnp.exp2((score - peak) * RATE)
                total = jnp.sum(p, axis=1, keepdims=True)
                mixed = jnp.dot(p.astype(BF), v, preferred_element_type=F32)
                out[pl.ds(start, HEAD), h * HEAD : (h + 1) * HEAD] = (mixed / total * keep).astype(BF)
            return carry

        lax.fori_loop(0, ROWS // HEAD, block, 0, unroll=2)

    @pl.when(pool == 1)
    def _():
        fresh_k[pl.ds(0, ROWS), :] = keys[...].astype(F32)
        fresh_v[pl.ds(0, ROWS), :] = values[...].astype(F32)
        out[...] = queries[...].astype(BF)
        query = lax.broadcasted_iota(jnp.int32, (HEAD, 3 * HEAD), 0)
        key = lax.broadcasted_iota(jnp.int32, (HEAD, 3 * HEAD), 1)
        row = jnp.bitwise_and(query, 7)
        step = jnp.right_shift(query, 5)
        newer = key - 2 * HEAD
        mine = (key < 2 * HEAD) & (jnp.right_shift(key, 5) == row)
        mine = mine | (
            (key >= 2 * HEAD)
            & (newer < 32)
            & (jnp.bitwise_and(newer, 7) == row)
            & (jnp.right_shift(newer, 3) <= step)
        )
        fence = jnp.where(mine, 0.0, MASKED)
        blank = jnp.zeros((96, HEAD), BF)
        quarter = jnp.right_shift(lax.broadcasted_iota(jnp.int32, (8, HEAD), 1), 5)

        def block(b, carry):
            start = pl.multiple_of(b * 8, 8)
            pages = [cache[lookup[b * 16 + i]] for i in range(16)]
            news = [pl.ds(u * DROWS + start, 8) for u in range(STEPS)]
            new_k = jnp.concatenate([fresh_k[n, :] for n in news], axis=0).astype(BF)
            new_v = jnp.concatenate([fresh_v[n, :] for n in news], axis=0).astype(BF)
            k = jnp.concatenate([page[:, :HEAD] for page in pages] + [new_k, blank], axis=0)
            v = jnp.concatenate([page[:, HEAD:] for page in pages] + [new_v, blank], axis=0)
            q = jnp.concatenate(
                [queries[n, h * HEAD : (h + 1) * HEAD] for n in news for h in range(4)], axis=0
            ).astype(BF)
            score = lax.dot_general(q, k, dims, preferred_element_type=F32)
            score = score + (fence + stored_bias[b])
            peak = jnp.max(score, axis=1, keepdims=True)
            p = jnp.exp2((score - peak) * RATE)
            total = jnp.sum(p, axis=1, keepdims=True)
            mixed = jnp.dot(p.astype(BF), v, preferred_element_type=F32) / total
            height = jnp.broadcast_to(peak + jnp.log2(total) / RATE, (HEAD, HEAD))
            for u in range(STEPS):
                lift = None
                for h in range(4):
                    at = (u * 4 + h) * 8
                    acc[news[u], h * HEAD : (h + 1) * HEAD] = mixed[at : at + 8]
                    lift = height[at : at + 8] if h == 0 else jnp.where(quarter == h, height[at : at + 8], lift)
                level[news[u], :] = lift
            return carry

        lax.fori_loop(0, DROWS // 8, block, 0, unroll=8)
        acc_out[...] = acc[...].astype(BF)


def attend(place, lookup, order, rows, weights, *arrays):
    smem, vm = pl.BlockSpec(memory_space=pltpu.SMEM), pl.BlockSpec(memory_space=pltpu.VMEM)
    return pl.pallas_call(
        attend_kernel,
        out_shape=[
            jax.ShapeDtypeStruct((ROWS, QCOLS), BF),
            jax.ShapeDtypeStruct((ROWS, QCOLS), BF),
            jax.ShapeDtypeStruct((ROWS, HEAD), F32),
        ],
        in_specs=[smem] * 3 + [pl.BlockSpec(memory_space=pl.ANY)] * (2 + len(arrays)),
        out_specs=[vm] * 3,
        scratch_shapes=[
            *[pltpu.VMEM(x.shape, x.dtype) for x in arrays],
            pltpu.VMEM((KPART, HALF, KW), BF),
            pltpu.VMEM((KPART, KW, QCOLS), BF),
            pltpu.VMEM((ROWS, QCOLS), F32),
            pltpu.VMEM((ROWS, QCOLS), F32),
            pltpu.VMEM((ROWS + HEAD, HEAD), F32),
            pltpu.VMEM((ROWS + HEAD, HEAD), F32),
            pltpu.SemaphoreType.DMA((KPART,)),
            pltpu.SemaphoreType.DMA((KPART,)),
            pltpu.SemaphoreType.DMA((len(arrays),)),
        ],
        compiler_params=pltpu.CompilerParams(vmem_limit_bytes=BIG),
        cost_estimate=pl.CostEstimate(flops=1 << 33, bytes_accessed=32 << 20, transcendentals=1 << 21),
        name="attend",
    )(place, lookup, order, rows, weights, *arrays)


def finish_kernel(place, *refs):
    sources, out, held, (masks, wide, tall_k, sems) = refs[:6], refs[6], refs[7:13], refs[13:]
    first, acc, level, arrived, source, prompt_bias = held
    pool = place[10]

    @pl.when(pool == 0)
    def _():
        bring(sources[:1], held[:1], sems)
        out[...] = first[...]

    @pl.when(pool == 1)
    def _():
        bring([*sources[:3], sources[3].at[pl.ds(0, ROWS), :], *sources[4:]], held, sems)
        dims = (((1,), (1,)), ((), ()))
        picks = source[...]
        for c in range(GROUPS):
            masks[:, c * HEAD : (c + 1) * HEAD] = jnp.where(picks == c, 1.0, 0.0).astype(BF)
            tall_k[:, c * HEAD : (c + 1) * HEAD] = arrived[c * HEAD : (c + 1) * HEAD, :HEAD]
        bias = prompt_bias[...]
        for u in range(STEPS):
            rows = slice(u * DROWS, (u + 1) * DROWS)
            for h in range(4):
                lanes = slice(h * HEAD, (h + 1) * HEAD)
                q = first[rows, lanes]
                here = slice(h * DROWS, (h + 1) * DROWS)
                for c in range(GROUPS):
                    block = slice(c * HEAD, (c + 1) * HEAD)
                    wide[here, block] = q * masks[:, block]
                score = lax.dot_general(wide[here, :], tall_k[...], dims, preferred_element_type=F32) + bias
                before = level[rows, h * 32 : h * 32 + 1]
                peak = jnp.maximum(before, jnp.max(score, axis=1, keepdims=True))
                p = jnp.exp2((score - peak) * RATE)
                fade = jnp.exp2((before - peak) * RATE)
                total = fade + jnp.sum(p, axis=1, keepdims=True)
                p = p.astype(BF)
                spread = jnp.concatenate(
                    [p * masks[:, c * HEAD : (c + 1) * HEAD] for c in range(GROUPS)], axis=1
                )
                mixed = acc[rows, lanes].astype(F32) * fade
                mixed = mixed + jnp.dot(spread, arrived[:, HEAD:], preferred_element_type=F32)
                out[rows, lanes] = (mixed / total).astype(BF)


def finish(place, *arrays):
    anywhere = pl.BlockSpec(memory_space=pl.ANY)
    held = [pltpu.VMEM(x.shape if x.shape[0] <= ROWS else (ROWS, x.shape[1]), x.dtype) for x in arrays]
    return pl.pallas_call(
        finish_kernel,
        out_shape=jax.ShapeDtypeStruct((ROWS, QCOLS), BF),
        in_specs=[pl.BlockSpec(memory_space=pltpu.SMEM)] + [anywhere] * len(arrays),
        out_specs=pl.BlockSpec(memory_space=pltpu.VMEM),
        scratch_shapes=[
            *held,
            pltpu.VMEM((DROWS, ROWS), BF),
            pltpu.VMEM((4 * DROWS, ROWS), BF),
            pltpu.VMEM((HEAD, ROWS), BF),
            pltpu.SemaphoreType.DMA((len(arrays),)),
        ],
        compiler_params=pltpu.CompilerParams(vmem_limit_bytes=BIG),
        cost_estimate=pl.CostEstimate(flops=1 << 31, bytes_accessed=8 << 20, transcendentals=1 << 20),
        name="finish",
    )(place, *arrays)


def prefill_layout(page_req, req_len):
    count = page_req.shape[0]
    index = jnp.arange(count, dtype=jnp.int32)
    same = page_req[:, None] == page_req[None, :]
    first = jnp.min(jnp.where(same, index[None, :], count), axis=1)
    owner = jnp.repeat(page_req, PAGE)
    place = jnp.arange(count * PAGE, dtype=jnp.int32) - jnp.repeat(first, PAGE) * PAGE
    match = owner[:, None] == jnp.arange(req_len.shape[0], dtype=jnp.int32)[None, :]
    lengths = jnp.sum(jnp.where(match, req_len[None, :], 0), axis=1)
    return owner, place, place < lengths


def decode_layout(row_src, assign, req_len, group):
    slots = jnp.arange(GROUPS, dtype=jnp.int32)
    table = assign.reshape(GROUPS, GROUPS)
    chosen = jnp.sum(jnp.where(table == group, slots[None, :], 0), axis=1)
    requests = slots * GROUPS + chosen
    catalog = jnp.arange(req_len.shape[0], dtype=jnp.int32)
    lengths = jnp.sum(jnp.where(requests[:, None] == catalog[None, :], req_len[None, :], 0), axis=1)
    pick = row_src[:, None] == slots[None, :]
    return jnp.sum(jnp.where(pick, lengths[None, :], 0), axis=1)


def first_pages(page_req, assign, group):
    slots = jnp.arange(GROUPS, dtype=jnp.int32)
    table = assign.reshape(GROUPS, GROUPS)
    mine = jnp.sum(jnp.where((slots == group)[:, None], table, 0), axis=0)
    local = page_req - group * GROUPS
    starts = jnp.sum((local[None, :] < slots[:, None]).astype(jnp.int32), axis=1)
    target = mine[None, :] == slots[:, None]
    return jnp.sum(jnp.where(target, starts[None, :], 0), axis=1)


def shards(
    hidden_rows,
    w_query,
    key_matrix,
    value_matrix,
    resident_cache,
    page_req,
    req_len,
    assign,
    row_src,
    resident_length,
    page_lookup,
):
    group = lax.axis_index("grp")
    tp = lax.axis_index("tp")
    pool = lax.axis_index("pool")
    y = lax.rem(group, 4)
    x_lo, z = tp // RING, lax.rem(tp, RING)
    half = lax.rem(y, 2)
    send = lambda value, axis, pairs: lax.ppermute(value, axis, pairs)

    with jax.named_scope("rows"):
        rings = [[x * RING + i for i in range(RING)] for x in range(2)]
        rows = lax.all_gather(hidden_rows[0], "tp", axis=0, tiled=True, axis_index_groups=rings)

    owner, prefill_place, usable = prefill_layout(page_req, req_len)
    prompt_length = decode_layout(row_src, assign, req_len, group)
    decode_place = (
        (prompt_length + resident_length)[None, :] + jnp.arange(STEPS, dtype=jnp.int32)[:, None]
    ).reshape(-1)
    positions = jnp.where(pool == 0, prefill_place, decode_place)
    freqs = jnp.exp(jnp.arange(HEAD // 2, dtype=F32) * (-2.0 * math.log(THETA) / HEAD))
    angles = positions.astype(F32)[:, None] * freqs[None, :]
    cosine, sine = jnp.cos(angles), jnp.sin(angles)
    cosine = jnp.concatenate([cosine, cosine], axis=1)
    sine = jnp.concatenate([-sine, sine], axis=1)
    owners = owner.reshape(GROUPS, HEAD)
    prior = jnp.concatenate([jnp.full((1, HEAD), -1, jnp.int32), owners[:-1]], axis=0)
    seen_owner = jnp.concatenate([prior, owners], axis=1)
    i = jnp.arange(HEAD, dtype=jnp.int32)[:, None]
    k = jnp.arange(2 * HEAD, dtype=jnp.int32)[None, :] - HEAD
    allowed = (owners[:, :, None] == seen_owner[:, None, :]) & (k <= i)[None]
    seen = jnp.where(allowed, 0.0, MASKED).astype(F32)
    usable_rows = jnp.broadcast_to(usable.astype(F32)[:, None], (ROWS, HEAD))
    stored_ok = jnp.arange(32, dtype=jnp.int32)[None, :] < resident_length[:, None]
    stored_bias = jnp.where(stored_ok, 0.0, MASKED).astype(F32).reshape(DROWS // 8, 1, 2 * HEAD)
    stored_bias = jnp.concatenate([stored_bias, jnp.zeros((DROWS // 8, 1, HEAD), F32)], axis=2)
    prompt_ok = jnp.arange(HEAD, dtype=jnp.int32)[None, :] < prompt_length[:, None]
    prompt_bias = jnp.where(prompt_ok, 0.0, MASKED).astype(F32)
    source = jnp.broadcast_to(row_src[:, None], (DROWS, HEAD))
    place = jnp.concatenate(
        [jnp.stack([z, x_lo]), first_pages(page_req, assign, group), pool[None]]
    ).astype(jnp.int32)
    lookup = page_lookup.reshape(-1)
    tables = (cosine, sine, seen, usable_rows, stored_bias, prompt_bias, source, place, lookup)

    with jax.named_scope("weights"):
        own_weight = (w_query, key_matrix.T, value_matrix.T)
        offsets = jnp.stack([half * 4 + pool, half * 4 + 2 + pool]).astype(jnp.int32)
        piece0, piece1 = cut(offsets, *own_weight, tables)
        swap_core = [(0, 1), (1, 0)]
        a0 = send(piece0, "tp", flip(8))
        a1 = send(piece1, ("pool", "grp", "tp"), far_x())
        b0 = send(a0, "grp", ring_y(-1))
        b1 = send(a1, "grp", ring_y(1))
        parts = [a0, a1, b0, b1] + [send(v, "pool", swap_core) for v in (a0, a1, b0, b1)]
        order = []
        for h, p in ((half, pool), (1 - half, pool), (half, 1 - pool), (1 - half, 1 - pool)):
            order += [h * 4 + p, h * 4 + 2 + p]
        order = jnp.stack(order).astype(jnp.int32)

    own_kv, side_kv = project_tall(order, rows, own_weight[1], own_weight[2], parts)
    pair = send(own_kv, "tp", flip(1))
    side = send(side_kv, "tp", flip(8))
    diag = send(side_kv, "tp", flip(9))
    other_query = project_query(order, rows, parts)
    side_query = send(other_query, "tp", flip(8))
    keys, values, bins = make_keys(place, other_query, own_kv, pair, side, diag, cosine, sine)
    arrived = lax.all_to_all(bins, ("pool", "grp"), split_axis=0, concat_axis=0, tiled=True)
    first, acc, level = attend(
        place,
        lookup,
        order,
        rows,
        w_query,
        side_query,
        cosine,
        sine,
        keys,
        values,
        stored_bias,
        seen,
        usable_rows,
        resident_cache,
    )
    return finish(
        place, first, acc, level, arrived.reshape(2 * ROWS, 2 * HEAD), source, prompt_bias
    )[None]


def solution(mesh):
    return jax.shard_map(
        shards,
        mesh=mesh,
        in_specs=(
            P("pool", ("grp", "tp"), None),
            P(None, "tp"),
            P(None, "tp"),
            P(None, "tp"),
            P("grp", None, "tp"),
            P("grp"),
            P(),
            P(),
            P("grp"),
            P("grp"),
            P("grp", None),
        ),
        out_specs=P("pool", "grp", "tp"),
        check_vma=False,
    )
```

profile of v0, /device:TPU:1, one launch (start us, length us, event | category | flops | bytes accessed | tf_op | source)
XLA Modules:
  0.0 182.1 jit_solution(2931263871024201548)
XLA Ops:
  8.0 0.8 lt.68
  8.9 0.8 select_reduce_fusion.3
  9.8 0.8 select_reduce_fusion.2
  12.0 0.7 broadcast_in_dim.183
  17.0 1.9 %fusion = (f32[1024,64]{1,0:T(8,128)S(1)}, f32[1024,64]{1,0:T(8,128)S(1)}, f32[1024,64]{1,0:T(8,128)S(1)}) fusion(f32[64]{0:T(128)S(1)} %multiply_exponential_fusion, f32[1024]{0:T(1024)S(1)} %select_convert_fusion), kind=kLoop, calls=%fused_computation.7 | loop fusion | flops 131072 | bytes 790784 | tf_op jit(solution)/shard_map/neg | solution.py:541
  18.9 1.3 pad_maximum_fusion
  20.3 0.7 fusion.1.refs_5_
  21.0 1.2 and_select_fusion.refs_2_.refs_6_
  22.2 0.8 broadcast_in_dim.196.refs_6_.refs_4_
  23.0 1.0 broadcast_in_dim.191.refs_3_.refs_7_
  24.0 3.9 %cut.1 = (bf16[1280,512]{1,0:T(8,128)(2,1)}, bf16[1280,512]{1,0:T(8,128)(2,1)}) custom-call(s32[2]{0:T(128)} %pad_add_fusion.1.offsets, bf16[8192,512]{1,0:T(8,128)(2,1)} %weights.1, bf16[64,8192]{1,0:T(8,128)(2,1)} %bitcast.23, bf16[64,8192]{1,0:T(8,128)(2,1)} %bitcast.25, f32[1024,128]{1,0:T(8,128)} %get-tuple-element.30.refs_0_.refs_4_.refs_1_, ...), custom_call_target="tpu_custom_call" | custom-call | bytes 5242880 | tf_op jit(solution)/shard_map/weights/cut/pallas_call | solution.py:91
  27.9 2.0 %collective-permute-start = (bf16[1280,512]{1,0:T(8,128)(2,1)}, bf16[1280,512]{1,0:T(8,128)(2,1)S(1)}, u32[]{:S(2)}, u32[]{:S(2)}) collective-permute-start(bf16[1280,512]{1,0:T(8,128)(2,1)} %get-tuple-element.15), channel_id=1, source_target_pairs={{0,8},{1,9},{2,10},{3,11},{4,12},{5,13},{6,14},{7,15},{8,0},{9,1},... | collective-permute-start | bytes 3932168 | tf_op jit(solution)/shard_map/weights/ppermute | solution.py:525
  30.0 1.8 collective-permute-start.1
  31.8 25.7 %collective-permute-done.refs_0_ = bf16[1280,512]{1,0:T(8,128)(2,1)S(1)} collective-permute-done((bf16[1280,512]{1,0:T(8,128)(2,1)}, bf16[1280,512]{1,0:T(8,128)(2,1)S(1)}, u32[]{:S(2)}, u32[]{:S(2)}) %collective-permute-start) | collective-permute-done | bytes 1310752 | tf_op jit(solution)/shard_map/weights/ppermute | solution.py:525
  57.4 4.0 %collective-permute-start.2 = (bf16[1280,512]{1,0:T(8,128)(2,1)S(1)}, bf16[1280,512]{1,0:T(8,128)(2,1)}, u32[]{:S(2)}, u32[]{:S(2)}) collective-permute-start(bf16[1280,512]{1,0:T(8,128)(2,1)S(1)} %collective-permute-done.refs_0_), channel_id=1, source_target_pairs={{0,48},{16,0},{32,16},{48,32},{64,112},{80,64},{96,80},{112,96},{1... | collective-permute-start | bytes 3932168 | tf_op jit(solution)/shard_map/weights/ppermute | solution.py:525
  62.1 2.0 %collective-permute-start.4 = (bf16[1280,512]{1,0:T(8,128)(2,1)S(1)}, bf16[1280,512]{1,0:T(8,128)(2,1)}, u32[]{:S(2)}, u32[]{:S(2)}) collective-permute-start(bf16[1280,512]{1,0:T(8,128)(2,1)S(1)} %collective-permute-done.refs_0_), channel_id=1, source_target_pairs={{0,128},{128,0},{1,129},{129,1},{2,130},{130,2},{3,131},{131,3},{4... | collective-permute-start | bytes 3932168 | tf_op jit(solution)/shard_map/weights/ppermute | solution.py:525
  64.2 23.9 %collective-permute-done.2.refs_2_ = bf16[1280,512]{1,0:T(8,128)(2,1)} collective-permute-done((bf16[1280,512]{1,0:T(8,128)(2,1)S(1)}, bf16[1280,512]{1,0:T(8,128)(2,1)}, u32[]{:S(2)}, u32[]{:S(2)}) %collective-permute-start.2) | collective-permute-done | bytes 1310752 | tf_op jit(solution)/shard_map/weights/ppermute | solution.py:525
  88.1 2.4 %collective-permute-start.6 = (bf16[1280,512]{1,0:T(8,128)(2,1)}, bf16[1280,512]{1,0:T(8,128)(2,1)}, u32[]{:S(2)}, u32[]{:S(2)}) collective-permute-start(bf16[1280,512]{1,0:T(8,128)(2,1)} %collective-permute-done.2.refs_2_), channel_id=1, source_target_pairs={{0,128},{128,0},{1,129},{129,1},{2,130},{130,2},{3,131},{131,3},{4... | collective-permute-start | bytes 3932168 | tf_op jit(solution)/shard_map/weights/ppermute | solution.py:525
  90.4 0.9 collective-permute-done.3.refs_3_
  91.3 2.6 %collective-permute-start.7 = (bf16[1280,512]{1,0:T(8,128)(2,1)}, bf16[1280,512]{1,0:T(8,128)(2,1)}, u32[]{:S(2)}, u32[]{:S(2)}) collective-permute-start(bf16[1280,512]{1,0:T(8,128)(2,1)} %collective-permute-done.3.refs_3_), channel_id=1, source_target_pairs={{0,128},{128,0},{1,129},{129,1},{2,130},{130,2},{3,131},{131,3},{4... | collective-permute-start | bytes 3932168 | tf_op jit(solution)/shard_map/weights/ppermute | solution.py:525
  94.6 2.3 %collective-permute-done.7.refs_7_ = bf16[1280,512]{1,0:T(8,128)(2,1)} collective-permute-done((bf16[1280,512]{1,0:T(8,128)(2,1)}, bf16[1280,512]{1,0:T(8,128)(2,1)}, u32[]{:S(2)}, u32[]{:S(2)}) %collective-permute-start.7) | collective-permute-done | bytes 1310752 | tf_op jit(solution)/shard_map/weights/ppermute | solution.py:525
  97.0 10.2 %all-gather.3.cloned.1.call-done = bf16[1,512,8192]{2,1,0:T(8,128)(2,1)} async-done(((bf16[1,64,8192]{2,1,0:T(8,128)(2,1)}), bf16[1,512,8192]{2,1,0:T(8,128)(2,1)}) %all-gather.3.cloned.1.call-update) | async-done | bytes 8388624 | tf_op jit(solution)/shard_map/rows/all_gather | solution.py:529
  107.1 8.9 %project_tall.1 = (bf16[512,128]{1,0:T(8,128)(2,1)}, bf16[512,128]{1,0:T(8,128)(2,1)}) custom-call(s32[8]{0:T(128)} %stack.48.order, bf16[512,8192]{1,0:T(8,128)(2,1)} %bitcast.20, bf16[64,8192]{1,0:T(8,128)(2,1)} %bitcast.24, bf16[64,8192]{1,0:T(8,128)(2,1)} %bitcast.26, bf16[1280,512]{1,0:T(8,128)(2,1)} %copy-done, bf16[1280,512]{1,0:T(8,128)(2,1)} %copy-done.1, ...), custom_call_target="tpu_custom_call" | custom-call | flops 2147483648 | bytes 12582912 | tf_op jit(solution)/shard_map/project_tall/pallas_call | solution.py:146
  116.5 1.1 collective-permute-start.10
  117.5 1.2 collective-permute-start.9
  118.7 8.6 %project_query.1.refs_6_ = bf16[512,512]{1,0:T(8,128)(2,1)} custom-call(s32[8]{0:T(128)} %stack.48.order, bf16[512,8192]{1,0:T(8,128)(2,1)} %bitcast.21, bf16[1280,512]{1,0:T(8,128)(2,1)} %copy-done, bf16[1280,512]{1,0:T(8,128)(2,1)} %copy-done.1, bf16[1280,512]{1,0:T(8,128)(2,1)} %collective-permute-done.2.refs_2_, ...), custom_call_target="tpu_custom_call" | custom-call | flops 4294967296 | bytes 16777216 | tf_op jit(solution)/shard_map/project_query/pallas_call | solution.py:187
  127.3 1.3 collective-permute-start.8
  129.9 3.8 %keys.1 = (bf16[1024,128]{1,0:T(8,128)(2,1)}, bf16[1024,128]{1,0:T(8,128)(2,1)}, bf16[16,128,256]{2,1,0:T(8,128)(2,1)}) custom-call(s32[11]{0:T(128)} %pad_add_fusion.refs_7_.place, bf16[512,128]{1,0:T(8,128)(2,1)} %get-tuple-element.17.refs_0_, bf16[512,128]{1,0:T(8,128)(2,1)} %copy-done.9, bf16[512,128]{1,0:T(8,128)(2,1)} %copy-done.8, ...), custom_call_target="tpu_custom_call" | custom-call | flops 8589934592 | bytes 4194304 | tf_op jit(solution)/shard_map/keys/pallas_call | solution.py:250
  133.8 8.2 %all-to-all-start = ((bf16[16,128,256]{2,1,0:T(8,128)(2,1)}), bf16[16,128,256]{2,1,0:T(8,128)(2,1)}, u32[]{:S(2)}, u32[]{:S(2)}) async-start(bf16[16,128,256]{2,1,0:T(8,128)(2,1)} %get-tuple-element.24), calls=%async_computation | async-start | bytes 2097152 | tf_op jit(solution)/shard_map/all_to_all | solution.py:584
  142.0 0.8 copy-done.6
  142.9 21.0 %attend.1 = (bf16[1024,512]{1,0:T(8,128)(2,1)}, bf16[1024,512]{1,0:T(8,128)(2,1)}, f32[1024,128]{1,0:T(8,128)}) custom-call(s32[11]{0:T(128)} %pad_add_fusion.refs_7_.place, s32[512]{0:T(512)} %reshape.157.refs_8_.lookup, s32[8]{0:T(128)} %stack.48.order, bf16[512,8192]{1,0:T(8,128)(2,1)} %bitcast.22, bf16[8192,512]{1,0:T(8,128)(2,1)} %weights.1, ...), custom_call_target="tpu_custom_call" | custom-call | flops 8589934592 | bytes 33554432 | tf_op jit(solution)/shard_map/attend/pallas_call | solution.py:382
  163.9 11.3 %finish.1 = bf16[1024,512]{1,0:T(8,128)(2,1)} custom-call(s32[11]{0:T(128)} %pad_add_fusion.refs_7_.place, bf16[1024,512]{1,0:T(8,128)(2,1)} %get-tuple-element.21.refs_0_, bf16[1024,512]{1,0:T(8,128)(2,1)} %get-tuple-element.22.refs_1_, f32[1024,128]{1,0:T(8,128)} %get-tuple-element.23.refs_2_, bf16[2048,256]{1,0:T(8,128)(2,1)} %bitcast.14.refs_3_, ...), custom_call_target="tpu_custom_call" | custom-call | flops 2147483648 | bytes 8388608 | tf_op jit(solution)/shard_map/finish/pallas_call | solution.py:455
  (72 shorter events, 10.4 us)
Async XLA Ops:
  6.5 10.3 %copy-start.5 = (s32[64]{0:T(128)S(1)}, s32[64]{0:T(128)}, u32[]{:S(2)}) copy-start(s32[64]{0:T(128)} %param.17) | copy-start | bytes 772
  6.5 6.6 %copy-start.2 = (s32[64]{0:T(128)S(1)}, s32[64]{0:T(128)}, u32[]{:S(2)}) copy-start(s32[64]{0:T(128)} %param.16) | copy-start | bytes 772
  6.5 7.3 %copy-start.4 = (s32[256,2]{0,1:T(2,128)S(1)}, s32[256,2]{0,1:T(2,128)}, u32[]{:S(2)}) copy-start(s32[256,2]{0,1:T(2,128)} %param.21) | copy-start | bytes 6148
  6.5 100.6 %all-gather.3.cloned.1.call-start = ((), (), s32[]{:S(2)}) async-start(), calls=%async_computation.1 | async-start | bytes 9437184 | tf_op jit(solution)/shard_map/rows/all_gather | solution.py:529
  18.9 3.3 %copy-start.3 = (s32[256]{0:T(256)S(1)}, s32[256]{0:T(256)}, u32[]{:S(2)}) copy-start(s32[256]{0:T(256)} %param.19) | copy-start | bytes 3076
  27.9 29.5 %collective-permute-start = (bf16[1280,512]{1,0:T(8,128)(2,1)}, bf16[1280,512]{1,0:T(8,128)(2,1)S(1)}, u32[]{:S(2)}, u32[]{:S(2)}) collective-permute-start(bf16[1280,512]{1,0:T(8,128)(2,1)} %get-tuple-element.15), channel_id=1, source_target_pairs={{0,8},{1,9},{2,10},{3,11},{4,12},{5,13},{6,14},{7,15},{8,0},{9,1},... | collective-permute-start | bytes 3932168 | tf_op jit(solution)/shard_map/weights/ppermute | solution.py:525
  30.0 31.5 %collective-permute-start.1 = (bf16[1280,512]{1,0:T(8,128)(2,1)}, bf16[1280,512]{1,0:T(8,128)(2,1)S(1)}, u32[]{:S(2)}, u32[]{:S(2)}) collective-permute-start(bf16[1280,512]{1,0:T(8,128)(2,1)} %get-tuple-element.16), channel_id=1, source_target_pairs={{0,72},{1,73},{2,74},{3,75},{4,76},{5,77},{6,78},{7,79},{8,64},{9,... | collective-permute-start | bytes 3932168 | tf_op jit(solution)/shard_map/weights/ppermute | solution.py:525
  57.4 4.7 %copy-start = (bf16[1280,512]{1,0:T(8,128)(2,1)}, bf16[1280,512]{1,0:T(8,128)(2,1)S(1)}, u32[]{:S(2)}) copy-start(bf16[1280,512]{1,0:T(8,128)(2,1)S(1)} %collective-permute-done.refs_0_) | copy-start | bytes 3932164
  57.4 30.6 %collective-permute-start.2 = (bf16[1280,512]{1,0:T(8,128)(2,1)S(1)}, bf16[1280,512]{1,0:T(8,128)(2,1)}, u32[]{:S(2)}, u32[]{:S(2)}) collective-permute-start(bf16[1280,512]{1,0:T(8,128)(2,1)S(1)} %collective-permute-done.refs_0_), channel_id=1, source_target_pairs={{0,48},{16,0},{32,16},{48,32},{64,112},{80,64},{96,80},{112,96},{1... | collective-permute-start | bytes 3932168 | tf_op jit(solution)/shard_map/weights/ppermute | solution.py:525
  61.5 33.2 %copy-start.1 = (bf16[1280,512]{1,0:T(8,128)(2,1)}, bf16[1280,512]{1,0:T(8,128)(2,1)S(1)}, u32[]{:S(2)}) copy-start(bf16[1280,512]{1,0:T(8,128)(2,1)S(1)} %collective-permute-done.1.refs_1_) | copy-start | bytes 3932164
  61.5 29.9 %collective-permute-start.3 = (bf16[1280,512]{1,0:T(8,128)(2,1)S(1)}, bf16[1280,512]{1,0:T(8,128)(2,1)}, u32[]{:S(2)}, u32[]{:S(2)}) collective-permute-start(bf16[1280,512]{1,0:T(8,128)(2,1)S(1)} %collective-permute-done.1.refs_1_), channel_id=1, source_target_pairs={{0,16},{16,32},{32,48},{48,0},{64,80},{80,96},{96,112},{112,64},{1... | collective-permute-start | bytes 3932168 | tf_op jit(solution)/shard_map/weights/ppermute | solution.py:525
  62.1 32.5 %collective-permute-start.4 = (bf16[1280,512]{1,0:T(8,128)(2,1)S(1)}, bf16[1280,512]{1,0:T(8,128)(2,1)}, u32[]{:S(2)}, u32[]{:S(2)}) collective-permute-start(bf16[1280,512]{1,0:T(8,128)(2,1)S(1)} %collective-permute-done.refs_0_), channel_id=1, source_target_pairs={{0,128},{128,0},{1,129},{129,1},{2,130},{130,2},{3,131},{131,3},{4... | collective-permute-start | bytes 3932168 | tf_op jit(solution)/shard_map/weights/ppermute | solution.py:525
  64.2 30.5 %collective-permute-start.5 = (bf16[1280,512]{1,0:T(8,128)(2,1)S(1)}, bf16[1280,512]{1,0:T(8,128)(2,1)}, u32[]{:S(2)}, u32[]{:S(2)}) collective-permute-start(bf16[1280,512]{1,0:T(8,128)(2,1)S(1)} %collective-permute-done.1.refs_1_), channel_id=1, source_target_pairs={{0,128},{128,0},{1,129},{129,1},{2,130},{130,2},{3,131},{131,3},{4... | collective-permute-start | bytes 3932168 | tf_op jit(solution)/shard_map/weights/ppermute | solution.py:525
  88.1 6.6 %collective-permute-start.6 = (bf16[1280,512]{1,0:T(8,128)(2,1)}, bf16[1280,512]{1,0:T(8,128)(2,1)}, u32[]{:S(2)}, u32[]{:S(2)}) collective-permute-start(bf16[1280,512]{1,0:T(8,128)(2,1)} %collective-permute-done.2.refs_2_), channel_id=1, source_target_pairs={{0,128},{128,0},{1,129},{129,1},{2,130},{130,2},{3,131},{131,3},{4... | collective-permute-start | bytes 3932168 | tf_op jit(solution)/shard_map/weights/ppermute | solution.py:525
  91.3 5.6 %collective-permute-start.7 = (bf16[1280,512]{1,0:T(8,128)(2,1)}, bf16[1280,512]{1,0:T(8,128)(2,1)}, u32[]{:S(2)}, u32[]{:S(2)}) collective-permute-start(bf16[1280,512]{1,0:T(8,128)(2,1)} %collective-permute-done.3.refs_3_), channel_id=1, source_target_pairs={{0,128},{128,0},{1,129},{129,1},{2,130},{130,2},{3,131},{131,3},{4... | collective-permute-start | bytes 3932168 | tf_op jit(solution)/shard_map/weights/ppermute | solution.py:525
  116.0 12.6 %collective-permute-start.11 = (bf16[512,128]{1,0:T(8,128)(2,1)}, bf16[512,128]{1,0:T(8,128)(2,1)S(1)}, u32[]{:S(2)}, u32[]{:S(2)}) collective-permute-start(bf16[512,128]{1,0:T(8,128)(2,1)} %get-tuple-element.18), channel_id=1, source_target_pairs={{0,9},{1,8},{2,11},{3,10},{4,13},{5,12},{6,15},{7,14},{8,1},{9,0},... | collective-permute-start | bytes 393224 | tf_op jit(solution)/shard_map/ppermute | solution.py:525
  116.5 12.1 %collective-permute-start.10 = (bf16[512,128]{1,0:T(8,128)(2,1)}, bf16[512,128]{1,0:T(8,128)(2,1)S(1)}, u32[]{:S(2)}, u32[]{:S(2)}) collective-permute-start(bf16[512,128]{1,0:T(8,128)(2,1)} %get-tuple-element.18), channel_id=1, source_target_pairs={{0,8},{1,9},{2,10},{3,11},{4,12},{5,13},{6,14},{7,15},{8,0},{9,1},... | collective-permute-start | bytes 393224 | tf_op jit(solution)/shard_map/ppermute | solution.py:525
  117.5 11.0 %collective-permute-start.9 = (bf16[512,128]{1,0:T(8,128)(2,1)}, bf16[512,128]{1,0:T(8,128)(2,1)S(1)}, u32[]{:S(2)}, u32[]{:S(2)}) collective-permute-start(bf16[512,128]{1,0:T(8,128)(2,1)} %get-tuple-element.17.refs_0_), channel_id=1, source_target_pairs={{0,1},{1,0},{2,3},{3,2},{4,5},{5,4},{6,7},{7,6},{8,9},{9,8},{10,11... | collective-permute-start | bytes 393224 | tf_op jit(solution)/shard_map/ppermute | solution.py:525
  127.3 14.7 %collective-permute-start.8 = (bf16[512,512]{1,0:T(8,128)(2,1)}, bf16[512,512]{1,0:T(8,128)(2,1)S(1)}, u32[]{:S(2)}, u32[]{:S(2)}) collective-permute-start(bf16[512,512]{1,0:T(8,128)(2,1)} %project_query.1.refs_6_), channel_id=1, source_target_pairs={{0,8},{1,9},{2,10},{3,11},{4,12},{5,13},{6,14},{7,15},{8,0},{9,1},... | collective-permute-start | bytes 1572872 | tf_op jit(solution)/shard_map/ppermute | solution.py:525
  128.6 0.6 copy-start.9
  128.6 0.7 copy-start.7
  129.3 0.6 copy-start.8
  133.8 30.1 %all-to-all-start = ((bf16[16,128,256]{2,1,0:T(8,128)(2,1)}), bf16[16,128,256]{2,1,0:T(8,128)(2,1)}, u32[]{:S(2)}, u32[]{:S(2)}) async-start(bf16[16,128,256]{2,1,0:T(8,128)(2,1)} %get-tuple-element.24), calls=%async_computation | async-start | bytes 2097152 | tf_op jit(solution)/shard_map/all_to_all | solution.py:584
  142.0 0.8 copy-start.6
Sparse Core Ops, SparseCore 0:
  9.2 97.9 all-gather.2
where the time goes:
time: 182 us
  waiting for transfers between devices  63.7 us (35%)
  Pallas kernels  57.5 us (32%)
  starting transfers between devices  27.8 us (15%)
  between operations  13.7 us (8%)
  local copies, waits for them, and re-layouts  9.97 us (5%)
  other arithmetic  9.43 us (5%)
    ppermute x12, waiting for transfers between devices, shards(): send = lambda value, axis, pairs: lax.ppermute(value, axis, pairs)  52.8 us
    pallas_call x1, Pallas kernels, attend(): pl.pallas_call(attend_kernel, out_shape=[jax.ShapeDtypeStruct((ROWS, QCOL...  21 us
    ppermute x12, starting transfers between devices, shards(): send = lambda value, axis, pairs: lax.ppermute(value, axis, pairs)  19.6 us
    pallas_call x1, Pallas kernels, finish(): pl.pallas_call(finish_kernel, out_shape=jax.ShapeDtypeStruct((ROWS, QCOLS...  11.3 us
    all_gather x1, waiting for transfers between devices, shards(): lax.all_gather(hidden_rows[0], 'tp', axis=0, tiled=True, axis_index_group...  10.2 us
    pallas_call x1, Pallas kernels, project_tall(): pl.pallas_call(tall_kernel, out_shape=[jax.ShapeDtypeStruct((HALF, HEAD),...  8.85 us
    pallas_call x1, Pallas kernels, project_query(): pl.pallas_call(query_kernel, out_shape=jax.ShapeDtypeStruct((HALF, QCOLS)...  8.58 us
    all_to_all x1, starting transfers between devices, shards(): lax.all_to_all(bins, ('pool', 'grp'), split_axis=0, concat_axis=0, tiled=...  8.23 us
  transfers between devices with their start and end apart: 14, of which 5 were waited for; matrix products, arithmetic and copies ran while one was open for 9% of the time, Pallas kernels for 21%

commit v1 on v0

--- a/solution.py
+++ b/solution.py
@@ -26,7 +26,7 @@
 ROWS = 1024
 DROWS = 256
 HALF = 512
-BIG = 63 << 20
+BIG = (64 << 20) - (192 << 10)
 BF = jnp.bfloat16
 F32 = jnp.float32
 
@@ -373,7 +373,7 @@
                 level[news[u], :] = lift
             return carry
 
-        lax.fori_loop(0, DROWS // 8, block, 0, unroll=8)
+        lax.fori_loop(0, DROWS // 8, block, 0, unroll=16)
         acc_out[...] = acc[...].astype(BF)
 
 
@@ -407,34 +407,48 @@
 
 
 def finish_kernel(place, *refs):
-    sources, out, held, (masks, wide, tall_k, sems) = refs[:6], refs[6], refs[7:13], refs[13:]
+    sources, out, held, (whole, masks, tall_k, sems, osems) = refs[:6], refs[6], refs[7:13], refs[13:]
     first, acc, level, arrived, source, prompt_bias = held
     pool = place[10]
 
     @pl.when(pool == 0)
     def _():
         bring(sources[:1], held[:1], sems)
-        out[...] = first[...]
+        copy = pltpu.make_async_copy(first, out, osems.at[0])
+        copy.start()
+        copy.wait()
 
     @pl.when(pool == 1)
     def _():
-        bring([*sources[:3], sources[3].at[pl.ds(0, ROWS), :], *sources[4:]], held, sems)
+        sources_here = [*sources[:3], sources[3].at[pl.ds(0, ROWS), :], *sources[4:]]
+        copies = [pltpu.make_async_copy(sources_here[i], held[i], sems.at[i]) for i in range(6)]
+        for i in (4, 3, 5, 0, 2, 1):
+            copies[i].start()
         dims = (((1,), (1,)), ((), ()))
+        copies[4].wait()
+        copies[3].wait()
         picks = source[...]
         for c in range(GROUPS):
             masks[:, c * HEAD : (c + 1) * HEAD] = jnp.where(picks == c, 1.0, 0.0).astype(BF)
             tall_k[:, c * HEAD : (c + 1) * HEAD] = arrived[c * HEAD : (c + 1) * HEAD, :HEAD]
+        for i in (5, 0, 2, 1):
+            copies[i].wait()
+        sent = [
+            pltpu.make_async_copy(
+                whole.at[pl.ds(u * DROWS, DROWS), :], out.at[pl.ds(u * DROWS, DROWS), :], osems.at[u]
+            )
+            for u in range(STEPS)
+        ]
         bias = prompt_bias[...]
         for u in range(STEPS):
             rows = slice(u * DROWS, (u + 1) * DROWS)
             for h in range(4):
                 lanes = slice(h * HEAD, (h + 1) * HEAD)
                 q = first[rows, lanes]
-                here = slice(h * DROWS, (h + 1) * DROWS)
-                for c in range(GROUPS):
-                    block = slice(c * HEAD, (c + 1) * HEAD)
-                    wide[here, block] = q * masks[:, block]
-                score = lax.dot_general(wide[here, :], tall_k[...], dims, preferred_element_type=F32) + bias
+                spread = jnp.concatenate(
+                    [q * masks[:, c * HEAD : (c + 1) * HEAD] for c in range(GROUPS)], axis=1
+                )
+                score = lax.dot_general(spread, tall_k[...], dims, preferred_element_type=F32) + bias
                 before = level[rows, h * 32 : h * 32 + 1]
                 peak = jnp.maximum(before, jnp.max(score, axis=1, keepdims=True))
                 p = jnp.exp2((score - peak) * RATE)
@@ -446,7 +460,10 @@
                 )
                 mixed = acc[rows, lanes].astype(F32) * fade
                 mixed = mixed + jnp.dot(spread, arrived[:, HEAD:], preferred_element_type=F32)
-                out[rows, lanes] = (mixed / total).astype(BF)
+                whole[rows, lanes] = (mixed / total).astype(BF)
+            sent[u].start()
+        for copy in sent:
+            copy.wait()
 
 
 def finish(place, *arrays):
@@ -456,13 +473,14 @@
         finish_kernel,
         out_shape=jax.ShapeDtypeStruct((ROWS, QCOLS), BF),
         in_specs=[pl.BlockSpec(memory_space=pltpu.SMEM)] + [anywhere] * len(arrays),
-        out_specs=pl.BlockSpec(memory_space=pltpu.VMEM),
+        out_specs=anywhere,
         scratch_shapes=[
             *held,
+            pltpu.VMEM((ROWS, QCOLS), BF),
             pltpu.VMEM((DROWS, ROWS), BF),
-            pltpu.VMEM((4 * DROWS, ROWS), BF),
             pltpu.VMEM((HEAD, ROWS), BF),
             pltpu.SemaphoreType.DMA((len(arrays),)),
+            pltpu.SemaphoreType.DMA((STEPS,)),
         ],
         compiler_params=pltpu.CompilerParams(vmem_limit_bytes=BIG),
         cost_estimate=pl.CostEstimate(flops=1 << 31, bytes_accessed=8 << 20, transcendentals=1 << 20),

time: 182 us -> 179 us (0.984)
  local copies, waits for them, and re-layouts: 9.97 us -> 7.76 us
    unnamed x22 -> x14, local copies, waits for them, and re-layouts: 2.31 us -> 0.16 us
  transfers between devices with their start and end apart: 14 -> 14, of which waited for: 5 -> 5; matrix products, arithmetic and copies ran while one was open for 9% -> 10% of each run, Pallas kernels for 21% -> 21%
where the time goes in v1:
time: 179 us
  waiting for transfers between devices  63.6 us (36%)
  Pallas kernels  56.6 us (32%)
  starting transfers between devices  27.8 us (16%)
  between operations  13.6 us (8%)
  other arithmetic  9.52 us (5%)
  local copies, waits for them, and re-layouts  7.76 us (4%)
    ppermute x12, waiting for transfers between devices, shards(): send = lambda value, axis, pairs: lax.ppermute(value, axis, pairs)  52.8 us
    pallas_call x1, Pallas kernels, attend(): pl.pallas_call(attend_kernel, out_shape=[jax.ShapeDtypeStruct((ROWS, QCOL...  20.8 us
    ppermute x12, starting transfers between devices, shards(): send = lambda value, axis, pairs: lax.ppermute(value, axis, pairs)  19.6 us
    pallas_call x1, Pallas kernels, finish(): pl.pallas_call(finish_kernel, out_shape=jax.ShapeDtypeStruct((ROWS, QCOLS...  10.6 us
    all_gather x1, waiting for transfers between devices, shards(): lax.all_gather(hidden_rows[0], 'tp', axis=0, tiled=True, axis_index_group...  10 us
    pallas_call x1, Pallas kernels, project_tall(): pl.pallas_call(tall_kernel, out_shape=[jax.ShapeDtypeStruct((HALF, HEAD),...  8.87 us
    pallas_call x1, Pallas kernels, project_query(): pl.pallas_call(query_kernel, out_shape=jax.ShapeDtypeStruct((HALF, QCOLS)...  8.59 us
    all_to_all x1, starting transfers between devices, shards(): lax.all_to_all(bins, ('pool', 'grp'), split_axis=0, concat_axis=0, tiled=...  8.23 us
  transfers between devices with their start and end apart: 14, of which 5 were waited for; matrix products, arithmetic and copies ran while one was open for 10% of the time, Pallas kernels for 21%

profile of v1, /device:TPU:1, one launch (start us, length us, event | category | flops | bytes accessed | tf_op | source)
XLA Modules:
  0.0 179.0 jit_solution(2718198111849772228)
XLA Ops:
  8.0 0.8 lt.68
  8.9 0.8 select_reduce_fusion.3
  9.8 0.8 select_reduce_fusion.2
  12.0 0.7 broadcast_in_dim.183
  14.0 0.7 reshape.157.refs_8_.lookup
  17.1 1.9 %fusion = (f32[1024,64]{1,0:T(8,128)S(1)}, f32[1024,64]{1,0:T(8,128)S(1)}, f32[1024,64]{1,0:T(8,128)S(1)}) fusion(f32[64]{0:T(128)S(1)} %multiply_exponential_fusion, f32[1024]{0:T(1024)S(1)} %select_convert_fusion), kind=kLoop, calls=%fused_computation.7 | loop fusion | flops 131072 | bytes 790784 | tf_op jit(solution)/shard_map/neg | solution.py:559
  19.0 1.4 pad_maximum_fusion
  20.4 0.7 fusion.1.refs_5_
  21.1 1.2 and_select_fusion.refs_2_.refs_6_
  22.3 0.8 broadcast_in_dim.196.refs_6_.refs_4_
  23.1 1.0 broadcast_in_dim.191.refs_3_.refs_7_
  24.1 4.0 %cut.1 = (bf16[1280,512]{1,0:T(8,128)(2,1)}, bf16[1280,512]{1,0:T(8,128)(2,1)}) custom-call(s32[2]{0:T(128)} %pad_add_fusion.1.offsets, bf16[8192,512]{1,0:T(8,128)(2,1)} %weights.1, bf16[64,8192]{1,0:T(8,128)(2,1)} %bitcast.23, bf16[64,8192]{1,0:T(8,128)(2,1)} %bitcast.25, f32[1024,128]{1,0:T(8,128)} %get-tuple-element.30.refs_0_.refs_4_.refs_1_, ...), custom_call_target="tpu_custom_call" | custom-call | bytes 5242880 | tf_op jit(solution)/shard_map/weights/cut/pallas_call | solution.py:91
  28.0 2.0 %collective-permute-start = (bf16[1280,512]{1,0:T(8,128)(2,1)}, bf16[1280,512]{1,0:T(8,128)(2,1)S(1)}, u32[]{:S(2)}, u32[]{:S(2)}) collective-permute-start(bf16[1280,512]{1,0:T(8,128)(2,1)} %get-tuple-element.15), channel_id=1, source_target_pairs={{0,8},{1,9},{2,10},{3,11},{4,12},{5,13},{6,14},{7,15},{8,0},{9,1},... | collective-permute-start | bytes 3932168 | tf_op jit(solution)/shard_map/weights/ppermute | solution.py:543
  30.1 1.8 %collective-permute-start.1 = (bf16[1280,512]{1,0:T(8,128)(2,1)}, bf16[1280,512]{1,0:T(8,128)(2,1)S(1)}, u32[]{:S(2)}, u32[]{:S(2)}) collective-permute-start(bf16[1280,512]{1,0:T(8,128)(2,1)} %get-tuple-element.16), channel_id=1, source_target_pairs={{0,72},{1,73},{2,74},{3,75},{4,76},{5,77},{6,78},{7,79},{8,64},{9,... | collective-permute-start | bytes 3932168 | tf_op jit(solution)/shard_map/weights/ppermute | solution.py:543
  31.9 25.7 %collective-permute-done.refs_0_ = bf16[1280,512]{1,0:T(8,128)(2,1)S(1)} collective-permute-done((bf16[1280,512]{1,0:T(8,128)(2,1)}, bf16[1280,512]{1,0:T(8,128)(2,1)S(1)}, u32[]{:S(2)}, u32[]{:S(2)}) %collective-permute-start) | collective-permute-done | bytes 1310752 | tf_op jit(solution)/shard_map/weights/ppermute | solution.py:543
  57.6 4.0 %collective-permute-start.2 = (bf16[1280,512]{1,0:T(8,128)(2,1)S(1)}, bf16[1280,512]{1,0:T(8,128)(2,1)}, u32[]{:S(2)}, u32[]{:S(2)}) collective-permute-start(bf16[1280,512]{1,0:T(8,128)(2,1)S(1)} %collective-permute-done.refs_0_), channel_id=1, source_target_pairs={{0,48},{16,0},{32,16},{48,32},{64,112},{80,64},{96,80},{112,96},{1... | collective-permute-start | bytes 3932168 | tf_op jit(solution)/shard_map/weights/ppermute | solution.py:543
  62.2 2.0 %collective-permute-start.4 = (bf16[1280,512]{1,0:T(8,128)(2,1)S(1)}, bf16[1280,512]{1,0:T(8,128)(2,1)}, u32[]{:S(2)}, u32[]{:S(2)}) collective-permute-start(bf16[1280,512]{1,0:T(8,128)(2,1)S(1)} %collective-permute-done.refs_0_), channel_id=1, source_target_pairs={{0,128},{128,0},{1,129},{129,1},{2,130},{130,2},{3,131},{131,3},{4... | collective-permute-start | bytes 3932168 | tf_op jit(solution)/shard_map/weights/ppermute | solution.py:543
  64.3 23.9 %collective-permute-done.2.refs_2_ = bf16[1280,512]{1,0:T(8,128)(2,1)} collective-permute-done((bf16[1280,512]{1,0:T(8,128)(2,1)S(1)}, bf16[1280,512]{1,0:T(8,128)(2,1)}, u32[]{:S(2)}, u32[]{:S(2)}) %collective-permute-start.2) | collective-permute-done | bytes 1310752 | tf_op jit(solution)/shard_map/weights/ppermute | solution.py:543
  88.2 2.4 %collective-permute-start.6 = (bf16[1280,512]{1,0:T(8,128)(2,1)}, bf16[1280,512]{1,0:T(8,128)(2,1)}, u32[]{:S(2)}, u32[]{:S(2)}) collective-permute-start(bf16[1280,512]{1,0:T(8,128)(2,1)} %collective-permute-done.2.refs_2_), channel_id=1, source_target_pairs={{0,128},{128,0},{1,129},{129,1},{2,130},{130,2},{3,131},{131,3},{4... | collective-permute-start | bytes 3932168 | tf_op jit(solution)/shard_map/weights/ppermute | solution.py:543
  90.6 0.9 collective-permute-done.3.refs_3_
  91.4 2.6 %collective-permute-start.7 = (bf16[1280,512]{1,0:T(8,128)(2,1)}, bf16[1280,512]{1,0:T(8,128)(2,1)}, u32[]{:S(2)}, u32[]{:S(2)}) collective-permute-start(bf16[1280,512]{1,0:T(8,128)(2,1)} %collective-permute-done.3.refs_3_), channel_id=1, source_target_pairs={{0,128},{128,0},{1,129},{129,1},{2,130},{130,2},{3,131},{131,3},{4... | collective-permute-start | bytes 3932168 | tf_op jit(solution)/shard_map/weights/ppermute | solution.py:543
  94.7 2.4 %collective-permute-done.7.refs_7_ = bf16[1280,512]{1,0:T(8,128)(2,1)} collective-permute-done((bf16[1280,512]{1,0:T(8,128)(2,1)}, bf16[1280,512]{1,0:T(8,128)(2,1)}, u32[]{:S(2)}, u32[]{:S(2)}) %collective-permute-start.7) | collective-permute-done | bytes 1310752 | tf_op jit(solution)/shard_map/weights/ppermute | solution.py:543
  97.1 10.0 %all-gather.3.cloned.1.call-done = bf16[1,512,8192]{2,1,0:T(8,128)(2,1)} async-done(((bf16[1,64,8192]{2,1,0:T(8,128)(2,1)}), bf16[1,512,8192]{2,1,0:T(8,128)(2,1)}) %all-gather.3.cloned.1.call-update) | async-done | bytes 8388624 | tf_op jit(solution)/shard_map/rows/all_gather | solution.py:547
  107.1 8.9 %project_tall.1 = (bf16[512,128]{1,0:T(8,128)(2,1)}, bf16[512,128]{1,0:T(8,128)(2,1)}) custom-call(s32[8]{0:T(128)} %stack.48.order, bf16[512,8192]{1,0:T(8,128)(2,1)} %bitcast.20, bf16[64,8192]{1,0:T(8,128)(2,1)} %bitcast.24, bf16[64,8192]{1,0:T(8,128)(2,1)} %bitcast.26, bf16[1280,512]{1,0:T(8,128)(2,1)} %copy-done, bf16[1280,512]{1,0:T(8,128)(2,1)} %copy-done.1, ...), custom_call_target="tpu_custom_call" | custom-call | flops 2147483648 | bytes 12582912 | tf_op jit(solution)/shard_map/project_tall/pallas_call | solution.py:146
  116.5 1.1 collective-permute-start.10
  117.6 1.2 collective-permute-start.9
  118.7 8.6 %project_query.1.refs_6_ = bf16[512,512]{1,0:T(8,128)(2,1)} custom-call(s32[8]{0:T(128)} %stack.48.order, bf16[512,8192]{1,0:T(8,128)(2,1)} %bitcast.21, bf16[1280,512]{1,0:T(8,128)(2,1)} %copy-done, bf16[1280,512]{1,0:T(8,128)(2,1)} %copy-done.1, bf16[1280,512]{1,0:T(8,128)(2,1)} %collective-permute-done.2.refs_2_, ...), custom_call_target="tpu_custom_call" | custom-call | flops 4294967296 | bytes 16777216 | tf_op jit(solution)/shard_map/project_query/pallas_call | solution.py:187
  127.3 1.3 collective-permute-start.8
  128.6 3.8 %keys.1 = (bf16[1024,128]{1,0:T(8,128)(2,1)}, bf16[1024,128]{1,0:T(8,128)(2,1)}, bf16[16,128,256]{2,1,0:T(8,128)(2,1)}) custom-call(s32[11]{0:T(128)} %pad_add_fusion.refs_7_.place, bf16[512,128]{1,0:T(8,128)(2,1)} %get-tuple-element.17.refs_0_, bf16[512,128]{1,0:T(8,128)(2,1)} %collective-permute-done.9.refs_1_, ...), custom_call_target="tpu_custom_call" | custom-call | flops 8589934592 | bytes 4194304 | tf_op jit(solution)/shard_map/keys/pallas_call | solution.py:250
  132.5 8.2 %all-to-all-start = ((bf16[16,128,256]{2,1,0:T(8,128)(2,1)}), bf16[16,128,256]{2,1,0:T(8,128)(2,1)}, u32[]{:S(2)}, u32[]{:S(2)}) async-start(bf16[16,128,256]{2,1,0:T(8,128)(2,1)} %get-tuple-element.24), calls=%async_computation | async-start | bytes 2097152 | tf_op jit(solution)/shard_map/all_to_all | solution.py:602
  140.7 20.8 %attend.1 = (bf16[1024,512]{1,0:T(8,128)(2,1)}, bf16[1024,512]{1,0:T(8,128)(2,1)}, f32[1024,128]{1,0:T(8,128)}) custom-call(s32[11]{0:T(128)} %pad_add_fusion.refs_7_.place, s32[512]{0:T(512)} %reshape.157.refs_8_.lookup, s32[8]{0:T(128)} %stack.48.order, bf16[512,8192]{1,0:T(8,128)(2,1)} %bitcast.22, bf16[8192,512]{1,0:T(8,128)(2,1)} %weights.1, ...), custom_call_target="tpu_custom_call" | custom-call | flops 8589934592 | bytes 33554432 | tf_op jit(solution)/shard_map/attend/pallas_call | solution.py:382
  161.5 10.6 %finish.1 = bf16[1024,512]{1,0:T(8,128)(2,1)} custom-call(s32[11]{0:T(128)} %pad_add_fusion.refs_7_.place, bf16[1024,512]{1,0:T(8,128)(2,1)} %get-tuple-element.21.refs_0_, bf16[1024,512]{1,0:T(8,128)(2,1)} %get-tuple-element.22.refs_1_, f32[1024,128]{1,0:T(8,128)} %get-tuple-element.23.refs_2_, bf16[2048,256]{1,0:T(8,128)(2,1)} %bitcast.14.refs_3_, ...), custom_call_target="tpu_custom_call" | custom-call | flops 2147483648 | bytes 8388608 | tf_op jit(solution)/shard_map/finish/pallas_call | solution.py:472
  (64 shorter events, 8.4 us)
Async XLA Ops:
  6.5 10.4 %copy-start.5 = (s32[64]{0:T(128)S(1)}, s32[64]{0:T(128)}, u32[]{:S(2)}) copy-start(s32[64]{0:T(128)} %param.17) | copy-start | bytes 772
  6.5 6.6 %copy-start.2 = (s32[64]{0:T(128)S(1)}, s32[64]{0:T(128)}, u32[]{:S(2)}) copy-start(s32[64]{0:T(128)} %param.16) | copy-start | bytes 772
  6.5 7.3 %copy-start.4 = (s32[256,2]{0,1:T(2,128)S(1)}, s32[256,2]{0,1:T(2,128)}, u32[]{:S(2)}) copy-start(s32[256,2]{0,1:T(2,128)} %param.21) | copy-start | bytes 6148
  6.5 100.6 %all-gather.3.cloned.1.call-start = ((), (), s32[]{:S(2)}) async-start(), calls=%async_computation.1 | async-start | bytes 9437184 | tf_op jit(solution)/shard_map/rows/all_gather | solution.py:547
  19.0 3.4 %copy-start.3 = (s32[256]{0:T(256)S(1)}, s32[256]{0:T(256)}, u32[]{:S(2)}) copy-start(s32[256]{0:T(256)} %param.19) | copy-start | bytes 3076
  28.0 29.5 %collective-permute-start = (bf16[1280,512]{1,0:T(8,128)(2,1)}, bf16[1280,512]{1,0:T(8,128)(2,1)S(1)}, u32[]{:S(2)}, u32[]{:S(2)}) collective-permute-start(bf16[1280,512]{1,0:T(8,128)(2,1)} %get-tuple-element.15), channel_id=1, source_target_pairs={{0,8},{1,9},{2,10},{3,11},{4,12},{5,13},{6,14},{7,15},{8,0},{9,1},... | collective-permute-start | bytes 3932168 | tf_op jit(solution)/shard_map/weights/ppermute | solution.py:543
  30.1 31.5 %collective-permute-start.1 = (bf16[1280,512]{1,0:T(8,128)(2,1)}, bf16[1280,512]{1,0:T(8,128)(2,1)S(1)}, u32[]{:S(2)}, u32[]{:S(2)}) collective-permute-start(bf16[1280,512]{1,0:T(8,128)(2,1)} %get-tuple-element.16), channel_id=1, source_target_pairs={{0,72},{1,73},{2,74},{3,75},{4,76},{5,77},{6,78},{7,79},{8,64},{9,... | collective-permute-start | bytes 3932168 | tf_op jit(solution)/shard_map/weights/ppermute | solution.py:543
  57.5 4.7 %copy-start = (bf16[1280,512]{1,0:T(8,128)(2,1)}, bf16[1280,512]{1,0:T(8,128)(2,1)S(1)}, u32[]{:S(2)}) copy-start(bf16[1280,512]{1,0:T(8,128)(2,1)S(1)} %collective-permute-done.refs_0_) | copy-start | bytes 3932164
  57.6 30.6 %collective-permute-start.2 = (bf16[1280,512]{1,0:T(8,128)(2,1)S(1)}, bf16[1280,512]{1,0:T(8,128)(2,1)}, u32[]{:S(2)}, u32[]{:S(2)}) collective-permute-start(bf16[1280,512]{1,0:T(8,128)(2,1)S(1)} %collective-permute-done.refs_0_), channel_id=1, source_target_pairs={{0,48},{16,0},{32,16},{48,32},{64,112},{80,64},{96,80},{112,96},{1... | collective-permute-start | bytes 3932168 | tf_op jit(solution)/shard_map/weights/ppermute | solution.py:543
  61.6 33.1 %copy-start.1 = (bf16[1280,512]{1,0:T(8,128)(2,1)}, bf16[1280,512]{1,0:T(8,128)(2,1)S(1)}, u32[]{:S(2)}) copy-start(bf16[1280,512]{1,0:T(8,128)(2,1)S(1)} %collective-permute-done.1.refs_1_) | copy-start | bytes 3932164
  61.6 29.9 %collective-permute-start.3 = (bf16[1280,512]{1,0:T(8,128)(2,1)S(1)}, bf16[1280,512]{1,0:T(8,128)(2,1)}, u32[]{:S(2)}, u32[]{:S(2)}) collective-permute-start(bf16[1280,512]{1,0:T(8,128)(2,1)S(1)} %collective-permute-done.1.refs_1_), channel_id=1, source_target_pairs={{0,16},{16,32},{32,48},{48,0},{64,80},{80,96},{96,112},{112,64},{1... | collective-permute-start | bytes 3932168 | tf_op jit(solution)/shard_map/weights/ppermute | solution.py:543
  62.2 32.5 %collective-permute-start.4 = (bf16[1280,512]{1,0:T(8,128)(2,1)S(1)}, bf16[1280,512]{1,0:T(8,128)(2,1)}, u32[]{:S(2)}, u32[]{:S(2)}) collective-permute-start(bf16[1280,512]{1,0:T(8,128)(2,1)S(1)} %collective-permute-done.refs_0_), channel_id=1, source_target_pairs={{0,128},{128,0},{1,129},{129,1},{2,130},{130,2},{3,131},{131,3},{4... | collective-permute-start | bytes 3932168 | tf_op jit(solution)/shard_map/weights/ppermute | solution.py:543
  64.3 30.4 %collective-permute-start.5 = (bf16[1280,512]{1,0:T(8,128)(2,1)S(1)}, bf16[1280,512]{1,0:T(8,128)(2,1)}, u32[]{:S(2)}, u32[]{:S(2)}) collective-permute-start(bf16[1280,512]{1,0:T(8,128)(2,1)S(1)} %collective-permute-done.1.refs_1_), channel_id=1, source_target_pairs={{0,128},{128,0},{1,129},{129,1},{2,130},{130,2},{3,131},{131,3},{4... | collective-permute-start | bytes 3932168 | tf_op jit(solution)/shard_map/weights/ppermute | solution.py:543
  88.2 6.5 %collective-permute-start.6 = (bf16[1280,512]{1,0:T(8,128)(2,1)}, bf16[1280,512]{1,0:T(8,128)(2,1)}, u32[]{:S(2)}, u32[]{:S(2)}) collective-permute-start(bf16[1280,512]{1,0:T(8,128)(2,1)} %collective-permute-done.2.refs_2_), channel_id=1, source_target_pairs={{0,128},{128,0},{1,129},{129,1},{2,130},{130,2},{3,131},{131,3},{4... | collective-permute-start | bytes 3932168 | tf_op jit(solution)/shard_map/weights/ppermute | solution.py:543
  91.4 5.6 %collective-permute-start.7 = (bf16[1280,512]{1,0:T(8,128)(2,1)}, bf16[1280,512]{1,0:T(8,128)(2,1)}, u32[]{:S(2)}, u32[]{:S(2)}) collective-permute-start(bf16[1280,512]{1,0:T(8,128)(2,1)} %collective-permute-done.3.refs_3_), channel_id=1, source_target_pairs={{0,128},{128,0},{1,129},{129,1},{2,130},{130,2},{3,131},{131,3},{4... | collective-permute-start | bytes 3932168 | tf_op jit(solution)/shard_map/weights/ppermute | solution.py:543
  116.0 12.6 %collective-permute-start.11 = (bf16[512,128]{1,0:T(8,128)(2,1)}, bf16[512,128]{1,0:T(8,128)(2,1)}, u32[]{:S(2)}, u32[]{:S(2)}) collective-permute-start(bf16[512,128]{1,0:T(8,128)(2,1)} %get-tuple-element.18), channel_id=1, source_target_pairs={{0,9},{1,8},{2,11},{3,10},{4,13},{5,12},{6,15},{7,14},{8,1},{9,0},... | collective-permute-start | bytes 393224 | tf_op jit(solution)/shard_map/ppermute | solution.py:543
  116.5 12.1 %collective-permute-start.10 = (bf16[512,128]{1,0:T(8,128)(2,1)}, bf16[512,128]{1,0:T(8,128)(2,1)}, u32[]{:S(2)}, u32[]{:S(2)}) collective-permute-start(bf16[512,128]{1,0:T(8,128)(2,1)} %get-tuple-element.18), channel_id=1, source_target_pairs={{0,8},{1,9},{2,10},{3,11},{4,12},{5,13},{6,14},{7,15},{8,0},{9,1},... | collective-permute-start | bytes 393224 | tf_op jit(solution)/shard_map/ppermute | solution.py:543
  117.6 11.1 %collective-permute-start.9 = (bf16[512,128]{1,0:T(8,128)(2,1)}, bf16[512,128]{1,0:T(8,128)(2,1)}, u32[]{:S(2)}, u32[]{:S(2)}) collective-permute-start(bf16[512,128]{1,0:T(8,128)(2,1)} %get-tuple-element.17.refs_0_), channel_id=1, source_target_pairs={{0,1},{1,0},{2,3},{3,2},{4,5},{5,4},{6,7},{7,6},{8,9},{9,8},{10,11... | collective-permute-start | bytes 393224 | tf_op jit(solution)/shard_map/ppermute | solution.py:543
  127.3 13.4 %collective-permute-start.8 = (bf16[512,512]{1,0:T(8,128)(2,1)}, bf16[512,512]{1,0:T(8,128)(2,1)}, u32[]{:S(2)}, u32[]{:S(2)}) collective-permute-start(bf16[512,512]{1,0:T(8,128)(2,1)} %project_query.1.refs_6_), channel_id=1, source_target_pairs={{0,8},{1,9},{2,10},{3,11},{4,12},{5,13},{6,14},{7,15},{8,0},{9,1},... | collective-permute-start | bytes 1572872 | tf_op jit(solution)/shard_map/ppermute | solution.py:543
  132.5 29.0 %all-to-all-start = ((bf16[16,128,256]{2,1,0:T(8,128)(2,1)}), bf16[16,128,256]{2,1,0:T(8,128)(2,1)}, u32[]{:S(2)}, u32[]{:S(2)}) async-start(bf16[16,128,256]{2,1,0:T(8,128)(2,1)} %get-tuple-element.24), calls=%async_computation | async-start | bytes 2097152 | tf_op jit(solution)/shard_map/all_to_all | solution.py:602
Sparse Core Ops, SparseCore 0:
  9.2 97.9 all-gather.2
